TPU v7x, 128 devices: a whole 4x4x4 slice. The times are simulated.
128 devices in a mesh: dp: 16 (over x_lo, z, core), mp: 8 (over x_hi, y).
Axes of the slice: x: 4 (x_hi: 2, x_lo: 2; x = x_hi * 2 + x_lo), y: 4, z: 4, core: 2. Of those that a mesh axis runs over, the one named last changes fastest.
Arguments:
- tokens: bfloat16 [16384, 2048], P('dp'), may hold values from -6 to 6
- lengths: int32 [16, 4], P('dp'), may hold values from 0 to 1024, as said below
- ln1_gain: float32 [2048], replicated, may hold values from 0.1 to 1.9
- ln1_bias: float32 [2048], replicated, may hold values from -4 to 4
- ln2_gain: float32 [2048], replicated, may hold values from 0.1 to 1.9
- ln2_bias: float32 [2048], replicated, may hold values from -4 to 4
- qkv_master: float32 [2048, 3, 2048], P(None, None, 'mp'), may hold values from -0.125 to 0.125
- qkv_bias: float32 [3, 2048], P(None, 'mp'), may hold values from -6 to 6
- out_master: float32 [2048, 2048], P('mp'), may hold values from -0.75 to 0.75
- up_master: float32 [2048, 8192], P(None, 'mp'), may hold values from -0.125 to 0.125
- up_bias: float32 [8192], P('mp'), may hold values from -6 to 6
- down_master: float32 [8192, 2048], P('mp'), may hold values from -0.0625 to 0.0625
- branch_bias: float32 [2048], replicated, may hold values from -4 to 4
- cotangent: bfloat16 [16384, 2048], P('dp'), may hold values from -6 to 6
Outputs:
- output: bfloat16 [16384, 2048], P('dp')
- grad_tokens: bfloat16 [16384, 2048], P('dp')
- grad_ln1_gain: float32 [2048], P('mp')
- grad_ln1_bias: float32 [2048], P('mp')
- grad_ln2_gain: float32 [2048], P('mp')
- grad_ln2_bias: float32 [2048], P('mp')
- grad_qkv: float32 [2048, 3, 2048], P('dp', None, 'mp')
- grad_qkv_bias: float32 [3, 2048], P(None, 'mp')
- grad_out: float32 [2048, 2048], P('mp', 'dp')
- grad_up: float32 [2048, 8192], P('dp', 'mp')
- grad_up_bias: float32 [8192], P('mp')
- grad_down: float32 [8192, 2048], P('mp', 'dp')
- grad_branch_bias: float32 [2048], P('mp')
Inputs may be any that keep to these rules, and one draw needn't show every extreme that they name: Row r of lengths describes bucket r: its sequences lie end to end from the bucket's first row in slot order and the rest of its 1024 rows are padding; a slot may be empty (length 0); each bucket's lengths sum to 512 or more; some bucket holds one sequence of exactly 1024.
All inputs are finite; a program needn't handle non-finite values.
Results may differ from a plain program's by a relative error of at most 0.012.
The roundings to bfloat16 on the way count: a program that leaves them out, or rounds other values in their place, can miss the bound.
Values may be sent and summed in bfloat16 or wider, within the bound.
A program may use at most 256 MiB of HBM per device.

v0:
```python
import math
from functools import partial

import jax
import jax.numpy as jnp
import numpy as np
from jax import lax
from jax.experimental import pallas as pl
from jax.experimental.pallas import tpu as pltpu
from jax.sharding import PartitionSpec as P

HS = 256
ROT = 64
BLK = 256
HALF = 128
SUB = 64
SLOTS = 2
BRANCH_CUT = 1280
NORM_CUT = 1280
OUT_CUT = 1280
GRAD_CUT = 1536
MESH = pl.DeviceIdType.MESH
MIB = 2**20
norm_eps = 1e-05
masked_value = -1e30
f32 = jnp.float32
bf16 = jnp.bfloat16


def dot_nn(a, b):
    return jnp.dot(a, b, preferred_element_type=f32)


def dot_nt(a, b):
    return lax.dot_general(a, b, (((1,), (1,)), ((), ())), preferred_element_type=f32)


def dot_tn(a, b):
    return lax.dot_general(a, b, (((0,), (0,)), ((), ())), preferred_element_type=f32)


def turn_off(k):
    return (2 + 3 * k + 3 * (k * (k - 1) // 2)) % 4


def in_turn(work, *after):
    @pl.loop(0, len(after))
    def _(k):
        work(turn_off(k))
        for i, actions in enumerate(after[:-1]):
            if actions:

                @pl.when(k == i)
                def _(actions=actions):
                    for action in actions:
                        action()

    for action in after[-1]:
        action()


def aligned(start, size, unit=None):
    if isinstance(start, int):
        return pl.ds(start, size)
    return pl.ds(pl.multiple_of(start, unit or size), size)


class Place:
    def __init__(self):
        self.dp = lax.axis_index("dp")
        self.mp = lax.axis_index("mp")
        self.x_hi = self.mp // 4
        self.y = self.mp % 4
        self.x_lo = self.dp // 8
        self.z = (self.dp // 2) % 4
        self.core = self.dp % 2

    def y_at(self, off):
        return (self.y + off) % 4

    def z_at(self, off):
        return (self.z + off) % 4

    def to_y(self, y):
        return (self.dp, self.x_hi * 4 + y)

    def ring_y(self):
        right, left = self.y_at(1), self.y_at(3)
        return self.y, right, self.y_at(2), left, self.to_y(right), self.to_y(left)

    def ring_z(self):
        right, left = self.z_at(1), self.z_at(3)
        return self.z, right, self.z_at(2), left, self.to_z(right), self.to_z(left)

    def to_x_hi(self):
        return (self.dp, (1 - self.x_hi) * 4 + self.y)

    def to_z(self, z):
        return ((self.x_lo * 4 + z) * 2 + self.core, self.mp)

    def to_x_lo(self):
        return (((1 - self.x_lo) * 4 + self.z) * 2 + self.core, self.mp)

    def to_core(self):
        return ((self.x_lo * 4 + self.z) * 2 + 1 - self.core, self.mp)


def greet(targets):
    for target in targets:
        pl.semaphore_signal(pltpu.get_barrier_semaphore(), inc=1, device_id=target, device_id_type=MESH)


def await_greetings(count):
    pl.semaphore_wait(pltpu.get_barrier_semaphore(), count)


class Link:
    def __init__(self, sems, number, src, dst, target):
        self.copy = pltpu.make_async_remote_copy(
            src_ref=src,
            dst_ref=dst,
            send_sem=sems.at[0, number],
            recv_sem=sems.at[1, number],
            device_id=target,
            device_id_type=MESH,
        )

    def start(self):
        self.copy.start()

    def got(self):
        self.copy.wait_recv()

    def sent(self):
        self.copy.wait_send()


class RingSum:
    def __init__(self, ring, src, at, buf, sems, base):
        self.src, self.at, self.buf = src, at, buf
        self.own, self.right, self.opp, self.left, to_right, to_left = ring
        part = lambda place, half: src.at[at(place, half)]
        self.links = [
            Link(sems, base + 0, part(self.opp, 0), buf.at[0], to_right),
            Link(sems, base + 1, part(self.opp, 1), buf.at[1], to_left),
            Link(sems, base + 2, part(self.right, 0), buf.at[2], to_right),
            Link(sems, base + 3, part(self.right, 1), buf.at[3], to_right),
            Link(sems, base + 4, part(self.left, 1), buf.at[4], to_left),
            Link(sems, base + 5, part(self.left, 0), buf.at[5], to_left),
        ]

    def send_opp(self):
        self.links[0].start()
        self.links[1].start()

    def send_right(self):
        self.links[3].start()

    def send_left(self):
        self.links[5].start()

    def relay(self):
        for number, place, half in ((0, self.right, 0), (1, self.left, 1)):
            self.links[number].got()
            at = self.at(place, half)
            self.src[at] = (self.src[at].astype(f32) + self.buf[number].astype(f32)).astype(bf16)
            self.links[2 if number == 0 else 4].start()

    def total(self, half):
        one, two = (2, 5) if half == 0 else (4, 3)
        self.links[one].got()
        self.links[two].got()
        own = self.src[self.at(self.own, half)].astype(f32)
        return own + self.buf[one].astype(f32) + self.buf[two].astype(f32)

    def finish(self):
        for link in self.links:
            link.sent()


class BucketSum:
    LINKS = 17

    def __init__(self, here, src, buf_wide, buf_cut, buf_x, buf_far, sems, width, cut):
        self.here, self.src, self.buf_x, self.buf_far, self.width, self.at_cut = here, src, buf_x, buf_far, width, cut
        self.cut, self.rest = pl.ds(0, cut), pl.ds(cut, width - cut)
        self.first_own = lambda y: y * BLK + here.x_hi * HALF
        self.first_far = lambda y: y * BLK + (1 - here.x_hi) * HALF

        def halves(first, cols):
            return lambda y, half: (aligned(first(y) + half * SUB, SUB), cols)

        self.far = RingSum(here.ring_y(), src, halves(self.first_far, self.cut), buf_cut, sems, 0)
        self.near = RingSum(here.ring_y(), src, halves(self.first_own, pl.ds(0, width)), buf_wide, sems, 6)
        self.across = [
            Link(
                sems,
                12 + off,
                src.at[aligned(self.first_far(here.y_at(off)), HALF), self.rest],
                buf_x.at[off],
                here.to_x_hi(),
            )
            for off in range(4)
        ]
        own_far = src.at[aligned(self.first_far(here.y), HALF), self.cut]
        self.last = Link(sems, 16, own_far, buf_far, here.to_x_hi())

    def add_across(self, off):
        self.across[off].got()
        rows = aligned(self.first_own(self.here.y_at(off)), HALF)
        self.src[rows, self.rest] = (
            self.src[rows, self.rest].astype(f32) + self.buf_x[off].astype(f32)
        ).astype(bf16)

    def pass_far(self):
        for half in range(2):
            self.src[self.far.at(self.here.y, half)] = self.far.total(half).astype(bf16)
        self.last.start()

    def total(self, half):
        if half == 0:
            self.last.got()
        near = self.near.total(half)
        far = self.buf_far[pl.ds(half * SUB, SUB), :].astype(f32)
        return jnp.concatenate([near[:, : self.at_cut] + far, near[:, self.at_cut :]], axis=1)

    def finish(self):
        self.far.finish()
        self.near.finish()
        for link in self.across:
            link.sent()
        self.last.sent()


class RingCopy:
    LINKS = 6

    def __init__(self, here, own, out, first, cols, sems, base):
        self.out, self.first, self.cols = out, first, cols
        own_y, right, _, left, to_right, to_left = here.ring_y()
        part = self.part
        halves = [own.at[pl.ds(half * SUB, SUB)] for half in range(2)]
        self.links = [
            Link(sems, base + 0, halves[0], part(own_y, 0), to_right),
            Link(sems, base + 1, halves[1], part(own_y, 1), to_left),
            Link(sems, base + 2, part(left, 0), part(left, 0), to_right),
            Link(sems, base + 3, part(right, 1), part(right, 1), to_left),
            Link(sems, base + 4, halves[1], part(own_y, 1), to_right),
            Link(sems, base + 5, halves[0], part(own_y, 0), to_left),
        ]

    def part(self, y, half=None, cols=None):
        if half is None:
            rows = aligned(self.first(y), HALF)
        else:
            rows = aligned(self.first(y) + half * SUB, SUB)
        return self.out.at[rows, self.cols if cols is None else cols]

    def start(self):
        for number in (0, 1, 4, 5):
            self.links[number].start()

    def pass_on(self):
        for near, far in ((0, 2), (1, 3)):
            self.links[near].got()
            self.links[far].start()

    def rest(self):
        self.links[4].got()
        self.links[5].got()

    def opposite(self):
        self.links[2].got()
        self.links[3].got()

    def finish(self):
        for link in self.links:
            link.sent()


class BucketCopy:
    LINKS = 18

    def __init__(self, here, own, out, sems, local_sem, width, cut):
        cut, rest = pl.ds(0, cut), pl.ds(cut, width - cut)
        first_own = lambda y: y * BLK + here.x_hi * HALF
        first_far = lambda y: y * BLK + (1 - here.x_hi) * HALF
        self.near = RingCopy(here, own, out, first_own, pl.ds(0, width), sems, 0)
        far_own = out.at[aligned(first_far(here.y), HALF), cut]
        self.far = RingCopy(here, far_own, out, first_far, cut, sems, RingCopy.LINKS)
        part = self.near.part
        y, right, opp, left, _, _ = here.ring_y()
        moves = [(own.at[:, cut], part(y, cols=cut)), (own.at[:, rest], part(y, cols=rest))]
        for place, half in ((left, None), (right, None), (opp, 0), (opp, 1)):
            moves.append((part(place, half, rest), part(place, half, rest)))
        self.across = [Link(sems, 2 * RingCopy.LINKS + i, src, dst, here.to_x_hi()) for i, (src, dst) in enumerate(moves)]
        self.keep = pltpu.make_async_copy(own, part(y), local_sem)

    def start(self):
        self.near.start()
        self.keep.start()

    def send_cut(self):
        self.across[0].start()

    def send_rest(self):
        self.across[1].start()

    def start_far(self):
        self.across[0].got()
        self.far.start()

    def pass_near(self):
        self.near.pass_on()

    def cross_near(self):
        self.near.rest()
        self.across[2].start()
        self.across[3].start()

    def cross_opp(self):
        for i in range(2):
            self.near.links[2 + i].got()
            self.across[4 + i].start()

    def pass_far(self):
        self.far.pass_on()

    def finish(self):
        self.far.rest()
        self.far.opposite()
        for link in self.across[1:]:
            link.got()
        for link in self.across:
            link.sent()
        self.near.finish()
        self.far.finish()
        self.keep.wait()


class GradSum:
    ORDER = (2, 1, 3, 0)
    LINKS = 15

    def __init__(self, here, grads, at, buf_core, buf_ring, buf_last, sems, free_sems):
        self.here, self.grads, self.buf_core, self.buf_last, self.free_sems = here, grads, buf_core, buf_last, free_sems
        self.at = lambda x_lo, z, core: at((x_lo * 4 + z) * 2 + core)
        self.cores = {
            off: [
                Link(
                    sems,
                    turn * 2 + x_lo,
                    grads.at[self.at(x_lo, here.z_at(off), 1 - here.core)],
                    buf_core.at[(turn % 2) * 2 + x_lo],
                    here.to_core(),
                )
                for x_lo in range(2)
            ]
            for turn, off in enumerate(self.ORDER)
        }
        self.ring = RingSum(here.ring_z(), grads, lambda z, half: self.at(half, z, here.core), buf_ring, sems, 8)
        self.other = self.at(1 - here.x_lo, here.z, here.core)
        self.last = Link(sems, 14, grads.at[self.other], buf_last, here.to_x_lo())

    def swap(self, off):
        turn = self.ORDER.index(off)
        if turn >= 2:
            pl.semaphore_wait(self.free_sems.at[turn % 2], 1)
        for link in self.cores[off]:
            link.start()

    def add_core(self, off):
        turn = self.ORDER.index(off)
        for x_lo in range(2):
            self.cores[off][x_lo].got()
            at = self.at(x_lo, self.here.z_at(off), self.here.core)
            self.grads[at] = (
                self.grads[at].astype(f32) + self.buf_core[(turn % 2) * 2 + x_lo].astype(f32)
            ).astype(bf16)
        if turn < 2:
            pl.semaphore_signal(
                self.free_sems.at[turn], inc=1, device_id=self.here.to_core(), device_id_type=MESH
            )

    def cross(self):
        low, high = self.ring.total(0), self.ring.total(1)
        mine = self.here.x_lo == 0
        self.grads[self.other] = jnp.where(mine, high, low).astype(bf16)
        self.last.start()
        return jnp.where(mine, low, high)

    def rest(self):
        self.last.got()
        return self.buf_last[...].astype(f32)

    def finish(self):
        for links in self.cores.values():
            for link in links:
                link.sent()
        self.last.sent()
        self.ring.finish()


class Total:
    def __init__(self, here, steps, bufs, sems):
        self.steps, self.bufs, self.at = steps, bufs, 0
        z_pair, y_pair = here.z + 1 - 2 * (here.z % 2), here.y + 1 - 2 * (here.y % 2)
        targets = [
            here.to_core(), here.to_z(z_pair), here.to_z(3 - here.z), here.to_x_lo(),
            here.to_y(y_pair), here.to_y(3 - here.y), here.to_x_hi(),
        ]
        self.links = [Link(sems, i, steps.at[i], bufs.at[i], target) for i, target in enumerate(targets)]

    def start(self):
        self.links[0].start()

    def step(self):
        i = self.at
        self.links[i].got()
        self.steps[i + 1] = self.steps[i] + self.bufs[i]
        self.at = i + 1
        if self.at < len(self.links):
            self.links[self.at].start()

    def finish(self):
        for link in self.links:
            link.sent()


def gelu_parts(v):
    cdf = 0.5 * (1.0 + lax.erf(v * (1.0 / math.sqrt(2.0))))
    slope = cdf + v * (jnp.exp(-0.5 * v * v) * (1.0 / math.sqrt(2.0 * math.pi)))
    return v * cdf, slope


def row_stats(load, width):
    tiles = width // 128
    total = load(0)
    for tile in range(1, tiles):
        total = total + load(tile)
    mean = jnp.sum(total, axis=-1, keepdims=True) * (1.0 / width)
    square = jnp.zeros_like(total)
    for tile in range(tiles):
        centred = load(tile) - mean
        square = square + centred * centred
    var = jnp.sum(square, axis=-1, keepdims=True) * (1.0 / width)
    return mean, lax.rsqrt(var + norm_eps)


def whole_kernel(
    lens, tok, cot, one_gain, one_bias, two_gain, two_bias, turn, freq, wq, bq, wo, wu, bu, wd, bb,
    out, gt, packed, tail, a_kept,
    tok_v, a_v, b_v, e_v, w_in, w_out, st, qkv_v, o_v, do_v, tabs, stats, g_v, du_v, rows_own, gt_own,
    z_wide, z_cut, z_x, z_far, s_wide, s_cut, s_x, s_far,
    one_core, one_ring, one_last, two_core, two_ring, two_last, steps, step_bufs,
    in_sems, st_sems, local_sems, z_sems, s_sems, out_sems, gt_sems, one_sems, two_sems, vec_sems, one_free, two_free,
):
    here = Place()
    rows_all, width = tok_v.shape
    hidden = g_v.shape[1]
    blocks = rows_all // BLK
    scale = 1.0 / math.sqrt(HS)
    qkv_first = hidden

    ring, ring_z = here.ring_y(), here.ring_z()
    greet([ring[4], ring[5], here.to_x_hi(), ring_z[4], ring_z[5], here.to_core(), here.to_x_lo()])

    def block_of(i):
        return pl.ds(i * BLK, BLK)

    def column(k):
        return pl.ds(k * HS, HS)

    tok_in = [pltpu.make_async_copy(tok.at[block_of(i)], tok_v.at[block_of(i)], in_sems.at[i]) for i in range(blocks)]
    cot_in = [pltpu.make_async_copy(cot.at[block_of(i)], e_v.at[block_of(i)], in_sems.at[blocks + i]) for i in range(blocks)]
    own_first = here.y * BLK + here.x_hi * HALF
    x_in = pltpu.make_async_copy(tok.at[aligned(own_first, HALF)], gt_own, in_sems.at[2 * blocks])
    turn_in = pltpu.make_async_copy(turn, tabs, in_sems.at[2 * blocks + 1])

    pieces = [((wq.at[j], (pl.ds(0, width),)),) for j in range(3)]
    pieces += [((wu.at[:, column(k)], (pl.ds(0, width),)),) for k in range(hidden // HS)]
    pieces += [tuple((wo.at[:, column(k)], (column(k),)) for k in range(width // HS))]
    pieces += [
        tuple((wd.at[:, column(k)], (pl.ds((k % 2) * hidden, hidden),)) for k in (2 * j, 2 * j + 1))
        for j in range(width // HS // 2)
    ]
    loads, number = [], 0
    for i, piece in enumerate(pieces):
        copies = []
        for src, (rows,) in piece:
            copies.append(pltpu.make_async_copy(src, st.at[i % SLOTS, rows], st_sems.at[number]))
            number += 1
        loads.append(copies)

    def load(i):
        if i < len(loads):
            for copy in loads[i]:
                copy.start()

    def take(i):
        for copy in loads[i]:
            copy.wait()
        slot = i % SLOTS
        if i < 7:
            first = qkv_first + i * HS if i < 3 else (i - 3) * HS

            @pl.loop(0, width // BLK)
            def _(r):
                rows = aligned(r * BLK, BLK)
                w_in[rows, pl.ds(first, HS)] = st[slot, rows, :].astype(bf16)

        elif i == 7:
            for k in range(width // HS):
                w_out[hidden:, column(k)] = st[slot, column(k), :].astype(bf16)
        else:
            for k in range(2):
                cols = column(2 * (i - 8) + k)

                @pl.loop(0, hidden // BLK)
                def _(r):
                    rows = aligned(r * BLK, BLK)
                    w_out[rows, cols] = st[slot, aligned(k * hidden + r * BLK, BLK), :].astype(bf16)

        load(i + SLOTS)

    tok_in[0].start()
    tok_in[1].start()
    for i in range(SLOTS):
        load(i)
    tok_in[2].start()
    turn_in.start()
    tok_in[3].start()

    end = []
    for j in range(4):
        end.append(lens[0, j] + (end[-1] if j else 0))

    def first_of(t):
        low = jnp.zeros_like(t)
        for j in range(4):
            low = jnp.where(t >= end[j], end[j], low)
        return low

    steps[0] = jnp.zeros(steps.shape[1:], f32)

    chunk = 64

    def norms(i):
        @pl.loop(0, BLK // chunk)
        def _(c):
            norm_chunk(aligned(i * BLK + c * chunk, chunk))

    def norm_chunk(rows):
        def tile_of(tile):
            return tok_v[rows, pl.ds(tile * 128, 128)].astype(f32)

        mean, rstd = row_stats(tile_of, width)
        stats[rows, 0:1] = mean
        stats[rows, 1:2] = rstd
        for tile in range(width // 128):
            cols = pl.ds(tile * 128, 128)
            normed = (tile_of(tile) - mean) * rstd
            a_v[rows, cols] = (normed * one_gain[:, cols] + one_bias[:, cols]).astype(bf16)
            b_v[rows, cols] = (normed * two_gain[:, cols] + two_bias[:, cols]).astype(bf16)

    def tables():
        starts = [jnp.int32(0)] + end[:3]
        lane_row = lax.broadcasted_iota(jnp.int32, (8, 128), 0)
        shift = jnp.zeros((8, 128), jnp.int32)
        for j in range(4):
            shift = jnp.where(lane_row == j, starts[j], shift)
        phase = shift.astype(f32) * freq[...]
        shift_cos, shift_sin = jnp.cos(phase), jnp.sin(phase)
        turn_in.wait()

        @pl.loop(0, rows_all // HALF)
        def _(i):
            rows = aligned(i * HALF, HALF)
            t = lax.broadcasted_iota(jnp.int32, (HALF, 128), 0) + i * HALF
            lane = lax.broadcasted_iota(jnp.int32, (HALF, 128), 1)
            c_of = jnp.broadcast_to(shift_cos[0:1], (HALF, 128))
            s_of = jnp.broadcast_to(shift_sin[0:1], (HALF, 128))
            for j in range(4):
                c_of = jnp.where(t >= end[j], shift_cos[j + 1 : j + 2], c_of)
                s_of = jnp.where(t >= end[j], shift_sin[j + 1 : j + 2], s_of)
            t_cos, t_sin = tabs[0, rows], tabs[1, rows]
            sin_of = t_sin * c_of - t_cos * s_of
            tabs[0, rows] = t_cos * c_of + t_sin * s_of
            tabs[1, rows] = jnp.where(lane < ROT // 2, -sin_of, sin_of)

    def turned(wide, sign, rows):
        low = wide[:, :128]
        lane = lax.broadcasted_iota(jnp.int32, low.shape, 1)
        other = jnp.where(lane < ROT // 2, pltpu.roll(low, 128 - ROT // 2, 1), pltpu.roll(low, ROT // 2, 1))
        low = low * tabs[0, rows] + sign * (other * tabs[1, rows])
        return jnp.concatenate([low, wide[:, 128:]], axis=1)

    def project(i):
        rows = aligned(i * BLK, BLK)
        mixed = dot_nn(a_v[rows, :], w_in[:, qkv_first:])
        for j in range(3):
            part = mixed[:, j * HS : (j + 1) * HS] + bq[j : j + 1, :]
            qkv_v[rows, column(j)] = (turned(part, 1.0, rows) if j < 2 else part).astype(bf16)

    def probabilities(first, seen):
        rows = aligned(first, BLK)
        t = lax.broadcasted_iota(jnp.int32, (BLK, 1), 0) + first
        key_at = lax.broadcasted_iota(jnp.int32, (BLK, seen), 1)
        scores = dot_nt(qkv_v[rows, :HS], qkv_v[:seen, HS : 2 * HS]) * scale
        scores = jnp.where((key_at >= first_of(t)) & (key_at <= t), scores, masked_value)
        weights = jnp.exp(scores - jnp.max(scores, axis=-1, keepdims=True))
        return weights * (1.0 / jnp.sum(weights, axis=-1, keepdims=True))

    def attend(off):
        first = here.y_at(off) * BLK
        probs = probabilities(first, rows_all).astype(bf16)
        o_v[aligned(first, BLK), :] = dot_nn(probs, qkv_v[:, 2 * HS :]).astype(bf16)

    def mask(i):
        rows = aligned(i * BLK, BLK)
        t = lax.broadcasted_iota(jnp.int32, (BLK, 1), 0) + i * BLK
        used = (t < end[3]).astype(f32)

        @pl.loop(0, width // 512)
        def _(c):
            cols = aligned(c * 512, 512)
            kept = e_v[rows, cols].astype(f32) * used
            e_v[rows, cols] = kept.astype(bf16)
            steps[0, 4:5, cols] += jnp.sum(kept, axis=0, keepdims=True)

    def mask_all():
        for copy in cot_in:
            copy.wait()
        pl.loop(0, blocks)(mask)

    def mixed_back():
        do_v[...] = dot_nt(e_v[...], w_out[hidden:, :]).astype(bf16)

    def attend_back(i):
        rows, seen = block_of(i), (i + 1) * BLK
        query, keys, values = qkv_v[rows, :HS], qkv_v[:seen, HS : 2 * HS], qkv_v[:seen, 2 * HS :]
        probs = probabilities(i * BLK, seen)
        grad_mixed = do_v[rows, :]
        grad_probs = dot_nt(grad_mixed, values)
        row_dot = jnp.sum(probs * grad_probs, axis=-1, keepdims=True)
        grad_scores = (probs * (grad_probs - row_dot)).astype(bf16)
        grad_query = dot_nn(grad_scores, keys) * scale
        grad_keys = dot_tn(grad_scores, query) * scale
        grad_values = dot_tn(probs.astype(bf16), grad_mixed)
        if i == blocks - 1:
            st[0, :seen] = grad_keys
            st[0, pl.ds(rows_all, seen)] = grad_values
        else:
            st[0, :seen] += grad_keys
            st[0, pl.ds(rows_all, seen)] += grad_values
        qkv_v[rows, :HS] = turned(grad_query, -1.0, rows).astype(bf16)

    def project_back():
        for i in range(blocks):
            rows = block_of(i)
            qkv_v[rows, HS : 2 * HS] = turned(st[0, rows], -1.0, rows).astype(bf16)
            qkv_v[rows, 2 * HS :] = st[0, pl.ds(rows_all + i * BLK, BLK)].astype(bf16)
            steps[0, 5:6, : 3 * HS] += jnp.sum(qkv_v[rows, :].astype(f32), axis=0, keepdims=True)

    z_v = a_v
    branch = BucketSum(here, z_v, z_wide, z_cut, z_x, z_far, z_sems, width, BRANCH_CUT)

    def feed_up(off):
        rows = aligned(here.y_at(off) * BLK, BLK)
        act, slope = gelu_parts(dot_nn(b_v[rows, :], w_in[:, :hidden]) + bu[...])
        g_v[rows, :] = act.astype(bf16)
        du_v[rows, :] = slope.astype(bf16)

    def feed_down(off):
        rows = aligned(here.y_at(off) * BLK, BLK)

        @pl.loop(0, 2)
        def _(c):
            cols = aligned(c * (width // 2), width // 2)
            z_v[rows, cols] = (
                dot_nn(o_v[rows, :], w_out[hidden:, cols]) + dot_nn(g_v[rows, :], w_out[:hidden, cols])
            ).astype(bf16)

    def out_rows():
        x_in.wait()
        t = lax.broadcasted_iota(jnp.int32, (SUB, 1), 0) + own_first
        for half in range(2):
            rows = pl.ds(half * SUB, SUB)
            used = (t + half * SUB < end[3]).astype(f32)
            rows_own[rows, :] = (used * (gt_own[rows, :].astype(f32) + branch.total(half) + bb[...])).astype(bf16)

    def attend_up(off):
        attend(off)
        feed_up(off)

    wide = BucketSum(here, tok_v, s_wide, s_cut, s_x, s_far, s_sems, width, NORM_CUT)

    def into_norms(off):
        rows = aligned(here.y_at(off) * BLK, BLK)
        grad_low = (dot_nt(e_v[rows, :], w_out[:hidden, :]) * du_v[rows, :].astype(f32)).astype(bf16)
        du_v[rows, :] = grad_low
        steps[0, 6:7, :hidden] += jnp.sum(grad_low.astype(f32), axis=0, keepdims=True)
        mean, rstd = stats[rows, 0:1], stats[rows, 1:2]

        @pl.loop(0, 4)
        def _(c):
            cols = aligned(c * (width // 4), width // 4)
            da = dot_nt(qkv_v[rows, :], w_in[cols, qkv_first:])
            db = dot_nt(du_v[rows, :], w_in[cols, :hidden])
            normed = (tok_v[rows, cols].astype(f32) - mean) * rstd
            steps[0, 0:1, cols] += jnp.sum(da * normed, axis=0, keepdims=True)
            steps[0, 1:2, cols] += jnp.sum(da, axis=0, keepdims=True)
            steps[0, 2:3, cols] += jnp.sum(db * normed, axis=0, keepdims=True)
            steps[0, 3:4, cols] += jnp.sum(db, axis=0, keepdims=True)
            tok_v[rows, cols] = (da * one_gain[:, cols] + db * two_gain[:, cols]).astype(bf16)

    def gt_rows():
        for half in range(2):
            rows = pl.ds(half * SUB, SUB)
            total = wide.total(half)
            x = gt_own[rows, :].astype(f32)
            centred = x - jnp.mean(x, axis=-1, keepdims=True)
            rstd = lax.rsqrt(jnp.mean(centred * centred, axis=-1, keepdims=True) + norm_eps)
            normed = centred * rstd
            grad = rstd * (
                total - jnp.mean(total, axis=-1, keepdims=True)
                - normed * jnp.mean(total * normed, axis=-1, keepdims=True)
            )
            gt_own[rows, :] = (e_v[aligned(own_first + half * SUB, SUB), :].astype(f32) + grad).astype(bf16)

    one = GradSum(
        here, w_in, lambda block: (aligned(block * HALF, HALF), pl.ds(0, w_in.shape[1])),
        one_core, one_ring, one_last, one_sems, one_free,
    )
    two = GradSum(
        here, w_out, lambda block: (pl.ds(0, w_out.shape[0]), aligned(block * HALF, HALF)),
        two_core, two_ring, two_last, two_sems, two_free,
    )

    def grads_one(off):
        @pl.loop(0, 2)
        def _(x_lo):
            m = aligned((x_lo * 4 + here.z_at(off)) * BLK, BLK)
            w_in[m, :hidden] = dot_tn(b_v[:, m], du_v[...]).astype(bf16)
            w_in[m, qkv_first:] = dot_tn(a_v[:, m], qkv_v[...]).astype(bf16)

    def grads_two(off):
        @pl.loop(0, 2)
        def _(x_lo):
            m = aligned((x_lo * 4 + here.z_at(off)) * BLK, BLK)
            w_out[:hidden, m] = dot_tn(g_v[...], e_v[:, m]).astype(bf16)
            w_out[hidden:, m] = dot_tn(o_v[...], e_v[:, m]).astype(bf16)

    def pack_one(part, add):
        for j in range(w_in.shape[1] // HS):
            rows = pl.ds(j * HALF, HALF)
            tile = part[:, j * HS : (j + 1) * HS]
            st[1, rows, :] = st[1, rows, :] + tile if add else tile

    def pack_two(part, add):
        tall = w_out.shape[0] // 2
        rows = pl.ds((w_in.shape[1] // HS) * HALF, tall)
        both = jnp.concatenate([part[:tall], part[tall:]], axis=1)
        st[1, rows, :] = st[1, rows, :] + both if add else both

    def cross_one():
        pack_one(one.cross(), False)

    def rest_one():
        pack_one(one.rest(), True)

    def cross_two():
        pack_two(two.cross(), False)

    def rest_two():
        pack_two(two.rest(), True)

    gather_out = BucketCopy(here, rows_own, out, out_sems, local_sems.at[1], width, OUT_CUT)
    gather_gt = BucketCopy(here, gt_own, gt, gt_sems, local_sems.at[2], width, GRAD_CUT)
    small = Total(here, steps, step_bufs, vec_sems)
    a_in = pltpu.make_async_copy(a_kept, a_v, local_sems.at[3])

    tok_in[0].wait()
    norms(0)
    take(0)
    tok_in[1].wait()
    norms(1)
    take(1)
    take(2)
    tables()
    tok_in[2].wait()
    norms(2)
    take(3)
    take(4)
    tok_in[3].wait()
    norms(3)
    take(5)
    take(6)
    a_out = pltpu.make_async_copy(a_v, a_kept, local_sems.at[0])
    a_out.start()

    @pl.loop(0, blocks)
    def _(i):
        project(i)

        @pl.when(i == 0)
        def _():
            take(7)

        @pl.when(i == 1)
        def _():
            take(8)

        @pl.when(i == 2)
        def _():
            take(9)

    def first_feed():
        take(11)
        for copy in cot_in + [x_in]:
            copy.start()
        await_greetings(7)
        a_out.wait()

    def feed(off):
        attend_up(off)
        pl.when(off == 2)(first_feed)
        feed_down(off)

    take(10)
    in_turn(
        feed,
        [branch.across[2].start, branch.far.send_opp],
        [branch.across[1].start, branch.far.send_right],
        [branch.across[3].start, branch.far.send_left, branch.far.relay],
        [branch.across[0].start],
    )
    mask_all()
    branch.add_across(2)
    branch.near.send_opp()
    mixed_back()
    attend_back(3)
    branch.add_across(1)
    branch.near.send_right()
    attend_back(2)
    branch.add_across(3)
    branch.near.send_left()
    attend_back(1)
    attend_back(0)
    project_back()
    branch.pass_far()
    in_turn(
        into_norms,
        [wide.across[2].start, wide.far.send_opp, branch.near.relay],
        [wide.across[1].start, wide.far.send_right],
        [wide.across[3].start, wide.far.send_left, partial(branch.add_across, 0)],
        [wide.across[0].start],
    )
    wide.far.relay()
    in_turn(
        grads_two,
        [partial(two.swap, 2), partial(wide.add_across, 2), wide.near.send_opp, small.start],
        [partial(two.swap, 1), out_rows, small.step, partial(two.add_core, 2), two.ring.send_opp, partial(two.add_core, 1), two.ring.send_right, gather_out.start, branch.finish, a_in.start, gather_out.send_rest, partial(wide.add_across, 1), wide.near.send_right, wide.pass_far, small.step],
        [partial(two.swap, 3), partial(wide.add_across, 3), wide.near.send_left, gather_out.send_cut, partial(two.add_core, 3), two.ring.send_left, small.step],
        [partial(two.swap, 0)],
    )
    two.ring.relay()
    wide.near.relay()
    a_in.wait()
    in_turn(
        grads_one,
        [partial(one.swap, 2), gather_out.pass_near, gather_out.cross_near],
        [partial(one.swap, 1), partial(wide.add_across, 0), small.step, partial(one.add_core, 2), one.ring.send_opp],
        [partial(one.swap, 3), gt_rows, gather_gt.send_cut, gather_gt.start, partial(one.add_core, 1), one.ring.send_right, partial(one.add_core, 3), one.ring.send_left, gather_out.cross_opp, partial(two.add_core, 0), small.step, cross_two, one.ring.relay, gather_out.start_far],
        [partial(one.swap, 0)],
    )
    gather_gt.pass_near()
    one.add_core(0)
    small.step()
    gather_gt.cross_near()
    gather_gt.start_far()
    gather_gt.send_rest()
    cross_one()
    gather_out.pass_far()
    gather_gt.pass_far()
    gather_gt.cross_opp()
    small.step()
    rest_two()
    rest_one()
    tail[...] = jnp.zeros_like(tail)
    tail[0:4, :HS] = steps[7, 0:4, aligned(here.mp * HS, HS)]
    tail[4:5, :HS] = steps[4, 4:5, aligned(here.mp * HS, HS)]
    tail[5:6, : 3 * HS] = steps[4, 5:6, : 3 * HS]
    tail[6:7, :hidden] = steps[4, 6:7, :hidden]
    packed_out = pltpu.make_async_copy(st.at[1, pl.ds(0, packed.shape[0])], packed, local_sems.at[4])
    packed_out.start()
    wide.finish()
    one.finish()
    two.finish()
    small.finish()
    gather_out.finish()
    gather_gt.finish()
    packed_out.wait()


def any_space():
    return pl.BlockSpec(memory_space=pl.ANY)


def vmem_space():
    return pl.BlockSpec(memory_space=pltpu.VMEM)


def rotary_tables(rows):
    inverse = np.exp(np.arange(ROT // 2) * (-2.0 * math.log(10000.0) / ROT))
    angle = np.arange(rows)[:, None] * inverse[None, :]
    cos_of, sin_of = np.ones((rows, 128)), np.zeros((rows, 128))
    freq = np.zeros((8, 128))
    for first in (0, ROT // 2):
        part = slice(first, first + ROT // 2)
        cos_of[:, part], sin_of[:, part] = np.cos(angle), np.sin(angle)
        freq[:, part] = inverse
    return np.stack([cos_of, sin_of]).astype(np.float32), freq.astype(np.float32)


def whole(lengths, tokens, cotangent, norms, wq, bq, wo, wu, bu, wd, bb):
    rows, width = tokens.shape
    hidden = wu.shape[1]
    turn, freq = rotary_tables(rows)
    shape = jax.ShapeDtypeStruct
    wide_in, tall_out = hidden + 3 * HS, hidden + HS
    outs = (
        shape((rows, width), bf16),
        shape((rows, width), bf16),
        shape((wide_in // HS * HALF + tall_out // 2, HS), f32),
        shape((8, hidden), f32),
        shape((rows, width), bf16),
    )
    v = pltpu.VMEM
    dma = pltpu.SemaphoreType.DMA

    def sum_bufs(cut):
        return [v((6, SUB, width), bf16), v((6, SUB, cut), bf16), v((4, HALF, width - cut), bf16), v((HALF, cut), bf16)]

    def grad_bufs(*part):
        return [v((4, *part), bf16), v((6, *part), bf16), v(part, bf16)]

    return pl.pallas_call(
        whole_kernel,
        out_shape=outs,
        in_specs=[
            pl.BlockSpec(memory_space=pltpu.SMEM), any_space(), any_space(), *[vmem_space()] * 4, any_space(),
            vmem_space(), any_space(), vmem_space(), any_space(), any_space(), vmem_space(), any_space(), vmem_space(),
        ],
        out_specs=(any_space(),) * 3 + (vmem_space(), any_space()),
        scratch_shapes=[
            v((rows, width), bf16), v((rows, width), bf16), v((rows, width), bf16), v((rows, width), bf16),
            v((width, wide_in), bf16), v((tall_out, width), bf16), v((SLOTS, width, HS), f32), v((rows, 3 * HS), bf16),
            v((rows, HS), bf16), v((rows, HS), bf16), v((2, rows, 128), f32), v((rows, 2), f32),
            v((rows, hidden), bf16), v((rows, hidden), bf16),
            v((HALF, width), bf16), v((HALF, width), bf16),
            *sum_bufs(BRANCH_CUT), *sum_bufs(NORM_CUT), *grad_bufs(HALF, wide_in), *grad_bufs(tall_out, HALF),
            v((8, 8, width), f32), v((7, 8, width), f32),
            dma((10,)), dma((23,)), dma((5,)), dma((2, BucketSum.LINKS)), dma((2, BucketSum.LINKS)),
            dma((2, BucketCopy.LINKS)), dma((2, BucketCopy.LINKS)), dma((2, GradSum.LINKS)), dma((2, GradSum.LINKS)),
            dma((2, 7)), pltpu.SemaphoreType.REGULAR((2,)), pltpu.SemaphoreType.REGULAR((2,)),
        ],
        compiler_params=pltpu.CompilerParams(
            collective_id=0, has_side_effects=True, vmem_limit_bytes=63 * MIB + 768 * 1024
        ),
        name="whole",
    )(lengths, tokens, cotangent, *norms, turn, freq, wq, bq, wo, wu, bu, wd, bb)


def finish_kernel(
    gathered, gathered_grad, packed, tail,
    output, grad_tokens, up, down, qkv, out, one_gain, one_bias, two_gain, two_bias, qkv_bias, up_bias, bias,
    wide_v, packed_v, tail_v, in_sems, out_sems,
):
    pieces = up.shape[1] // HS
    first = (pieces + 3) * HALF
    tall = (down.shape[0] + out.shape[0]) // 2
    over = down.shape[0] - tall
    left, right = pl.ds(0, HALF), pl.ds(HALF, HALF)
    parts = gathered.shape[0] // HALF
    moves, back = [(tail, tail_v), (packed, packed_v)], []
    for slot, (src, dst) in enumerate(((gathered, output), (gathered_grad, grad_tokens))):
        for k in range(parts):
            part = pl.ds(k * HALF, HALF)
            moves.append((src.at[part], wide_v.at[slot, part]))
            back.append((wide_v.at[slot, part], dst.at[part]))
    back += [(packed_v.at[pl.ds(j * HALF, HALF)], up.at[:, pl.ds(j * HS, HS)]) for j in range(pieces)]
    back += [(packed_v.at[pl.ds((pieces + j) * HALF, HALF)], qkv.at[j]) for j in range(3)]
    back += [
        (packed_v.at[pl.ds(first, tall), left], down.at[pl.ds(0, tall)]),
        (packed_v.at[pl.ds(first, over), right], down.at[pl.ds(tall, over)]),
        (packed_v.at[pl.ds(first + over, tall - over), right], out),
    ]
    loads = [pltpu.make_async_copy(src, dst, in_sems.at[i]) for i, (src, dst) in enumerate(moves)]
    stores = [pltpu.make_async_copy(src, dst, out_sems.at[i]) for i, (src, dst) in enumerate(back)]
    for copy in loads:
        copy.start()
    loads[0].wait()
    for row, ref in enumerate((one_gain, one_bias, two_gain, two_bias, bias)):
        ref[...] = tail_v[row, :HS]
    for j in range(3):
        qkv_bias[j : j + 1, :] = tail_v[5:6, pl.ds(j * HS, HS)]
    up_bias[...] = tail_v[6, :]
    loads[1].wait()
    for store in stores[2 * parts :]:
        store.start()
    for load, store in zip(loads[2:], stores):
        load.wait()
        store.start()
    for store in stores:
        store.wait()


def finish(gathered, gathered_grad, packed, tail):
    rows, width = gathered.shape
    hidden = tail.shape[1]
    shape = jax.ShapeDtypeStruct
    dma = pltpu.SemaphoreType.DMA
    moves = 2 * rows // HALF
    return pl.pallas_call(
        finish_kernel,
        out_shape=(
            shape(gathered.shape, bf16), shape(gathered.shape, bf16),
            shape((HALF, hidden), f32), shape((hidden, HALF), f32), shape((3, HALF, HS), f32), shape((HS, HALF), f32),
            shape((HS,), f32), shape((HS,), f32), shape((HS,), f32), shape((HS,), f32),
            shape((3, HS), f32), shape((hidden,), f32), shape((HS,), f32),
        ),
        in_specs=[any_space()] * 4,
        out_specs=(any_space(),) * 6 + (vmem_space(),) * 7,
        scratch_shapes=[
            pltpu.VMEM((2, rows, width), bf16), pltpu.VMEM(packed.shape, f32), pltpu.VMEM(tail.shape, f32),
            dma((moves + 2,)), dma((moves + hidden // HS + 6,)),
        ],
        compiler_params=pltpu.CompilerParams(vmem_limit_bytes=62 * MIB),
        name="finish",
    )(gathered, gathered_grad, packed, tail)


def local(
    tokens, lengths, ln1_gain, ln1_bias, ln2_gain, ln2_bias, qkv_master, qkv_bias, out_master, up_master, up_bias,
    down_master, branch_bias, cotangent,
):
    norms = [vector.reshape(1, -1) for vector in (ln1_gain, ln1_bias, ln2_gain, ln2_bias)]
    w_qkv = jnp.transpose(qkv_master, (1, 0, 2))
    gathered, gathered_grad, packed, tail, _ = whole(
        lengths, tokens, cotangent, norms, w_qkv, qkv_bias, out_master, up_master,
        up_bias.reshape(1, -1), down_master, branch_bias.reshape(1, -1),
    )
    (
        output, grad_tokens, up, down, qkv, out, one_gain, one_bias, two_gain, two_bias,
        qkv_bias_sum, up_bias_sum, bias_sum,
    ) = finish(gathered, gathered_grad, packed, tail)
    return (
        output,
        grad_tokens,
        one_gain,
        one_bias,
        two_gain,
        two_bias,
        jnp.transpose(qkv, (1, 0, 2)),
        qkv_bias_sum,
        out,
        up,
        up_bias_sum,
        down,
        bias_sum,
    )


def solution(mesh):
    placed = (
        P("dp", None),
        P("dp", None),
        P(),
        P(),
        P(),
        P(),
        P(None, None, "mp"),
        P(None, "mp"),
        P("mp", None),
        P(None, "mp"),
        P("mp"),
        P("mp", None),
        P(),
        P("dp", None),
    )
    return jax.shard_map(
        local,
        mesh=mesh,
        in_specs=placed,
        out_specs=(
            P("dp", None),
            P("dp", None),
            P("mp"),
            P("mp"),
            P("mp"),
            P("mp"),
            P("dp", None, "mp"),
            P(None, "mp"),
            P("mp", "dp"),
            P("dp", "mp"),
            P("mp"),
            P("mp", "dp"),
            P("mp"),
        ),
        check_vma=False,
    )
```

profile of v0, /device:TPU:0, one launch (start us, length us, event | category | flops | bytes accessed | tf_op | source)
XLA Modules:
  0.0 155.5 jit_solution(11064558212567264741)
XLA Ops:
  0.7 146.4 %whole.1 = (bf16[1024,2048]{1,0:T(8,128)(2,1)}, bf16[1024,2048]{1,0:T(8,128)(2,1)}, f32[1536,256]{1,0:T(8,128)}, f32[8,1024]{1,0:T(8,128)}, bf16[1024,2048]{1,0:T(8,128)(2,1)}) custom-call(s32[1,4]{1,0:T(1,128)} %lens.1, bf16[1024,2048]{1,0:T(8,128)(2,1)} %tok.1, bf16[1024,2048]{1,0:T(8,128)(2,1)} %cot.1, f32[1,2048]{1,0:T(1,128)} %bitcast.9, ...), custom_call_target="tpu_custom_call" | custom-call | tf_op jit(solution)/shard_map/whole/pallas_call | solution.py:948
  147.0 8.3 %finish.1 = (bf16[1024,2048]{1,0:T(8,128)(2,1)}, bf16[1024,2048]{1,0:T(8,128)(2,1)}, f32[128,1024]{1,0:T(8,128)}, f32[1024,128]{1,0:T(8,128)}, f32[3,128,256]{2,...) custom-call(bf16[1024,2048]{1,0:T(8,128)(2,1)} %get-tuple-element.30, ...), custom_call_target="tpu_custom_call" | custom-call | tf_op jit(solution)/shard_map/finish/pallas_call | solution.py:1025
where the time goes:
time: 156 us; the launch traced here: 155 us
  Pallas kernels  155 us (99%)
    pallas_call x1, Pallas kernels, whole(): pl.pallas_call(whole_kernel, out_shape=outs, in_specs=[pl.BlockSpec(memor...  146 us
    pallas_call x1, Pallas kernels, finish(): pl.pallas_call(finish_kernel, out_shape=(shape(gathered.shape, bf16), sha...  8.29 us

commit v1 on v0

--- a/solution.py
+++ b/solution.py
@@ -335,7 +335,6 @@
             link.sent()
         self.near.finish()
         self.far.finish()
-        self.keep.wait()
 
 
 class GradSum:
@@ -448,11 +447,12 @@
 
 
 def whole_kernel(
-    lens, tok, cot, one_gain, one_bias, two_gain, two_bias, turn, freq, wq, bq, wo, wu, bu, wd, bb,
-    out, gt, packed, tail, a_kept,
-    tok_v, a_v, b_v, e_v, w_in, w_out, st, qkv_v, o_v, do_v, tabs, stats, g_v, du_v, rows_own, gt_own,
+    lens, tok, cot, one_gain_h, one_bias_h, two_gain_h, two_bias_h, turn, freq_h, wq, bq_h, wo, wu, bu_h, wd, bb_h,
+    out, gt, packed, tail, b_v, e_v,
+    tail_v, tok_v, a_v, w_in, w_out, st, qkv_v, o_v, do_v, tabs, stats, g_v, du_v, rows_own, gt_own,
     z_wide, z_cut, z_x, z_far, s_wide, s_cut, s_x, s_far,
     one_core, one_ring, one_last, two_core, two_ring, two_last, steps, step_bufs,
+    one_gain, one_bias, two_gain, two_bias, freq, bq, bu, bb,
     in_sems, st_sems, local_sems, z_sems, s_sems, out_sems, gt_sems, one_sems, two_sems, vec_sems, one_free, two_free,
 ):
     here = Place()
@@ -523,7 +523,16 @@
 
         load(i + SLOTS)
 
+    small_pairs = [
+        (one_gain_h, one_gain), (one_bias_h, one_bias), (two_gain_h, two_gain), (two_bias_h, two_bias),
+        (freq_h, freq), (bq_h, bq), (bu_h, bu), (bb_h, bb),
+    ]
+    small_in = [
+        pltpu.make_async_copy(src, dst, in_sems.at[2 * blocks + 2 + i]) for i, (src, dst) in enumerate(small_pairs)
+    ]
     tok_in[0].start()
+    for copy in small_in:
+        copy.start()
     tok_in[1].start()
     for i in range(SLOTS):
         load(i)
@@ -546,8 +555,9 @@
     chunk = 64
 
     def norms(i):
-        @pl.loop(0, BLK // chunk)
-        def _(c):
+        rows = aligned(i * BLK, BLK)
+        pltpu.make_async_copy(tok.at[rows], tok_v.at[rows], in_sems.at[i]).wait()
+        for c in range(BLK // chunk):
             norm_chunk(aligned(i * BLK + c * chunk, chunk))
 
     def norm_chunk(rows):
@@ -778,49 +788,47 @@
     gather_out = BucketCopy(here, rows_own, out, out_sems, local_sems.at[1], width, OUT_CUT)
     gather_gt = BucketCopy(here, gt_own, gt, gt_sems, local_sems.at[2], width, GRAD_CUT)
     small = Total(here, steps, step_bufs, vec_sems)
-    a_in = pltpu.make_async_copy(a_kept, a_v, local_sems.at[3])
-
-    tok_in[0].wait()
-    norms(0)
-    take(0)
-    tok_in[1].wait()
-    norms(1)
-    take(1)
-    take(2)
-    tables()
-    tok_in[2].wait()
-    norms(2)
-    take(3)
-    take(4)
-    tok_in[3].wait()
-    norms(3)
-    take(5)
-    take(6)
-    a_out = pltpu.make_async_copy(a_v, a_kept, local_sems.at[0])
-    a_out.start()
+    a_in = pltpu.make_async_copy(tok, a_v, local_sems.at[3])
+
+    def renew():
+        a_in.wait()
+
+        @pl.loop(0, rows_all // chunk)
+        def _(c):
+            rows = aligned(c * chunk, chunk)
+            mean, rstd = stats[rows, 0:1], stats[rows, 1:2]
+            for tile in range(width // 128):
+                cols = pl.ds(tile * 128, 128)
+                normed = (a_v[rows, cols].astype(f32) - mean) * rstd
+                a_v[rows, cols] = (normed * one_gain[:, cols] + one_bias[:, cols]).astype(bf16)
+
+    for copy in small_in:
+        copy.wait()
+
+    def after_norms(i):
+        if i == 1:
+            tables()
+        for k in ((0,), (1, 2), (3, 4), (5, 6))[i]:
+            take(k)
+
+    @pl.loop(0, blocks)
+    def _(i):
+        norms(i)
+        for k in range(blocks):
+            pl.when(i == k)(partial(after_norms, k))
+
 
     @pl.loop(0, blocks)
     def _(i):
         project(i)
-
-        @pl.when(i == 0)
-        def _():
-            take(7)
-
-        @pl.when(i == 1)
-        def _():
-            take(8)
-
-        @pl.when(i == 2)
-        def _():
-            take(9)
+        for k in range(3):
+            pl.when(i == k)(partial(take, 7 + k))
 
     def first_feed():
         take(11)
         for copy in cot_in + [x_in]:
             copy.start()
         await_greetings(7)
-        a_out.wait()
 
     def feed(off):
         attend_up(off)
@@ -828,6 +836,24 @@
         feed_down(off)
 
     take(10)
+    out_done = pltpu.make_async_copy(out, e_v, local_sems.at[5])
+
+    def gt_copies(x_hi, first_sem):
+        parts = [aligned(y * BLK + x_hi * HALF, HALF) for y in range(4)]
+        return [pltpu.make_async_copy(gt.at[part], b_v.at[part], local_sems.at[first_sem + i]) for i, part in enumerate(parts)]
+
+    gt_near, gt_far = gt_copies(here.x_hi, 6), gt_copies(1 - here.x_hi, 10)
+
+    def finish_out():
+        gather_out.finish()
+        gather_out.keep.wait()
+        out_done.start()
+
+    def near_done():
+        gather_gt.keep.wait()
+        for copy in gt_near:
+            copy.start()
+
     in_turn(
         feed,
         [branch.across[2].start, branch.far.send_opp],
@@ -835,9 +861,9 @@
         [branch.across[3].start, branch.far.send_left, branch.far.relay],
         [branch.across[0].start],
     )
-    mask_all()
     branch.add_across(2)
     branch.near.send_opp()
+    mask_all()
     mixed_back()
     attend_back(3)
     branch.add_across(1)
@@ -851,56 +877,69 @@
     branch.pass_far()
     in_turn(
         into_norms,
-        [wide.across[2].start, wide.far.send_opp, branch.near.relay],
+        [wide.across[2].start, wide.far.send_opp, partial(branch.add_across, 0), branch.near.relay],
         [wide.across[1].start, wide.far.send_right],
-        [wide.across[3].start, wide.far.send_left, partial(branch.add_across, 0)],
+        [wide.across[3].start, wide.far.send_left],
         [wide.across[0].start],
     )
+    small.start()
+    wide.add_across(2)
+    wide.near.send_opp()
     wide.far.relay()
     in_turn(
         grads_two,
-        [partial(two.swap, 2), partial(wide.add_across, 2), wide.near.send_opp, small.start],
-        [partial(two.swap, 1), out_rows, small.step, partial(two.add_core, 2), two.ring.send_opp, partial(two.add_core, 1), two.ring.send_right, gather_out.start, branch.finish, a_in.start, gather_out.send_rest, partial(wide.add_across, 1), wide.near.send_right, wide.pass_far, small.step],
-        [partial(two.swap, 3), partial(wide.add_across, 3), wide.near.send_left, gather_out.send_cut, partial(two.add_core, 3), two.ring.send_left, small.step],
+        [partial(two.swap, 2), out_rows, small.step],
+        [partial(two.swap, 1), gather_out.start, gather_out.send_cut, branch.finish, a_in.start, partial(two.add_core, 2), two.ring.send_opp, partial(wide.add_across, 1), wide.near.send_right],
+        [partial(two.swap, 3), partial(two.add_core, 1), two.ring.send_right, partial(wide.add_across, 3), wide.near.send_left, renew],
         [partial(two.swap, 0)],
     )
-    two.ring.relay()
-    wide.near.relay()
-    a_in.wait()
+    wide.add_across(0)
+    small.step()
+    two.add_core(3)
+    two.ring.send_left()
+    wide.pass_far()
     in_turn(
         grads_one,
-        [partial(one.swap, 2), gather_out.pass_near, gather_out.cross_near],
-        [partial(one.swap, 1), partial(wide.add_across, 0), small.step, partial(one.add_core, 2), one.ring.send_opp],
-        [partial(one.swap, 3), gt_rows, gather_gt.send_cut, gather_gt.start, partial(one.add_core, 1), one.ring.send_right, partial(one.add_core, 3), one.ring.send_left, gather_out.cross_opp, partial(two.add_core, 0), small.step, cross_two, one.ring.relay, gather_out.start_far],
+        [partial(one.swap, 2)],
+        [partial(one.swap, 1), gather_out.send_rest, partial(one.add_core, 2), one.ring.send_opp, wide.near.relay, small.step, gather_out.pass_near, gather_out.cross_near, partial(two.add_core, 0)],
+        [partial(one.swap, 3), two.ring.relay, gt_rows, gather_gt.send_rest, gather_gt.send_cut, small.step, gather_gt.start, partial(one.add_core, 1), one.ring.send_right, partial(one.add_core, 3), one.ring.send_left, gather_out.start_far, cross_two],
         [partial(one.swap, 0)],
     )
+    small.step()
+    gather_out.cross_opp()
+    one.ring.relay()
+    gather_out.pass_far()
+    one.add_core(0)
     gather_gt.pass_near()
-    one.add_core(0)
-    small.step()
     gather_gt.cross_near()
     gather_gt.start_far()
-    gather_gt.send_rest()
+    small.step()
     cross_one()
-    gather_out.pass_far()
     gather_gt.pass_far()
     gather_gt.cross_opp()
+    near_done()
     small.step()
     rest_two()
     rest_one()
-    tail[...] = jnp.zeros_like(tail)
-    tail[0:4, :HS] = steps[7, 0:4, aligned(here.mp * HS, HS)]
-    tail[4:5, :HS] = steps[4, 4:5, aligned(here.mp * HS, HS)]
-    tail[5:6, : 3 * HS] = steps[4, 5:6, : 3 * HS]
-    tail[6:7, :hidden] = steps[4, 6:7, :hidden]
+    finish_out()
+    tail_v[...] = jnp.zeros_like(tail_v)
+    tail_v[0:4, :HS] = steps[7, 0:4, aligned(here.mp * HS, HS)]
+    tail_v[4:5, :HS] = steps[4, 4:5, aligned(here.mp * HS, HS)]
+    tail_v[5:6, : 3 * HS] = steps[4, 5:6, : 3 * HS]
+    tail_v[6:7, :hidden] = steps[4, 6:7, :hidden]
+    tail_out = pltpu.make_async_copy(tail_v, tail, local_sems.at[0])
+    tail_out.start()
     packed_out = pltpu.make_async_copy(st.at[1, pl.ds(0, packed.shape[0])], packed, local_sems.at[4])
     packed_out.start()
     wide.finish()
     one.finish()
     two.finish()
     small.finish()
-    gather_out.finish()
     gather_gt.finish()
-    packed_out.wait()
+    for copy in gt_far:
+        copy.start()
+    for copy in [tail_out, packed_out, out_done] + gt_near + gt_far:
+        copy.wait()
 
 
 def any_space():
@@ -934,7 +973,8 @@
         shape((rows, width), bf16),
         shape((wide_in // HS * HALF + tall_out // 2, HS), f32),
         shape((8, hidden), f32),
-        shape((rows, width), bf16),
+        pltpu.VMEM((rows, width), bf16),
+        pltpu.VMEM((rows, width), bf16),
     )
     v = pltpu.VMEM
     dma = pltpu.SemaphoreType.DMA
@@ -948,25 +988,23 @@
     return pl.pallas_call(
         whole_kernel,
         out_shape=outs,
-        in_specs=[
-            pl.BlockSpec(memory_space=pltpu.SMEM), any_space(), any_space(), *[vmem_space()] * 4, any_space(),
-            vmem_space(), any_space(), vmem_space(), any_space(), any_space(), vmem_space(), any_space(), vmem_space(),
-        ],
-        out_specs=(any_space(),) * 3 + (vmem_space(), any_space()),
+        in_specs=[pl.BlockSpec(memory_space=pltpu.SMEM)] + [any_space()] * 15,
+        out_specs=(any_space(),) * 4 + (vmem_space(),) * 2,
         scratch_shapes=[
-            v((rows, width), bf16), v((rows, width), bf16), v((rows, width), bf16), v((rows, width), bf16),
+            v((8, hidden), f32), v((rows, width), bf16), v((rows, width), bf16),
             v((width, wide_in), bf16), v((tall_out, width), bf16), v((SLOTS, width, HS), f32), v((rows, 3 * HS), bf16),
             v((rows, HS), bf16), v((rows, HS), bf16), v((2, rows, 128), f32), v((rows, 2), f32),
             v((rows, hidden), bf16), v((rows, hidden), bf16),
             v((HALF, width), bf16), v((HALF, width), bf16),
             *sum_bufs(BRANCH_CUT), *sum_bufs(NORM_CUT), *grad_bufs(HALF, wide_in), *grad_bufs(tall_out, HALF),
             v((8, 8, width), f32), v((7, 8, width), f32),
-            dma((10,)), dma((23,)), dma((5,)), dma((2, BucketSum.LINKS)), dma((2, BucketSum.LINKS)),
+            *[v((1, width), f32)] * 4, v((8, 128), f32), v((3, HS), f32), v((1, hidden), f32), v((1, width), f32),
+            dma((18,)), dma((23,)), dma((14,)), dma((2, BucketSum.LINKS)), dma((2, BucketSum.LINKS)),
             dma((2, BucketCopy.LINKS)), dma((2, BucketCopy.LINKS)), dma((2, GradSum.LINKS)), dma((2, GradSum.LINKS)),
             dma((2, 7)), pltpu.SemaphoreType.REGULAR((2,)), pltpu.SemaphoreType.REGULAR((2,)),
         ],
         compiler_params=pltpu.CompilerParams(
-            collective_id=0, has_side_effects=True, vmem_limit_bytes=63 * MIB + 768 * 1024
+            collective_id=0, has_side_effects=True, vmem_limit_bytes=55 * MIB + 768 * 1024
         ),
         name="whole",
     )(lengths, tokens, cotangent, *norms, turn, freq, wq, bq, wo, wu, bu, wd, bb)
@@ -975,7 +1013,7 @@
 def finish_kernel(
     gathered, gathered_grad, packed, tail,
     output, grad_tokens, up, down, qkv, out, one_gain, one_bias, two_gain, two_bias, qkv_bias, up_bias, bias,
-    wide_v, packed_v, tail_v, in_sems, out_sems,
+    packed_v, tail_v, in_sems, out_sems,
 ):
     pieces = up.shape[1] // HS
     first = (pieces + 3) * HALF
@@ -984,11 +1022,10 @@
     left, right = pl.ds(0, HALF), pl.ds(HALF, HALF)
     parts = gathered.shape[0] // HALF
     moves, back = [(tail, tail_v), (packed, packed_v)], []
-    for slot, (src, dst) in enumerate(((gathered, output), (gathered_grad, grad_tokens))):
+    for src, dst in ((gathered, output), (gathered_grad, grad_tokens)):
         for k in range(parts):
             part = pl.ds(k * HALF, HALF)
-            moves.append((src.at[part], wide_v.at[slot, part]))
-            back.append((wide_v.at[slot, part], dst.at[part]))
+            back.append((src.at[part], dst.at[part]))
     back += [(packed_v.at[pl.ds(j * HALF, HALF)], up.at[:, pl.ds(j * HS, HS)]) for j in range(pieces)]
     back += [(packed_v.at[pl.ds((pieces + j) * HALF, HALF)], qkv.at[j]) for j in range(3)]
     back += [
@@ -1000,6 +1037,8 @@
     stores = [pltpu.make_async_copy(src, dst, out_sems.at[i]) for i, (src, dst) in enumerate(back)]
     for copy in loads:
         copy.start()
+    for store in stores[: 2 * parts]:
+        store.start()
     loads[0].wait()
     for row, ref in enumerate((one_gain, one_bias, two_gain, two_bias, bias)):
         ref[...] = tail_v[row, :HS]
@@ -1008,9 +1047,6 @@
     up_bias[...] = tail_v[6, :]
     loads[1].wait()
     for store in stores[2 * parts :]:
-        store.start()
-    for load, store in zip(loads[2:], stores):
-        load.wait()
         store.start()
     for store in stores:
         store.wait()
@@ -1033,12 +1069,17 @@
         in_specs=[any_space()] * 4,
         out_specs=(any_space(),) * 6 + (vmem_space(),) * 7,
         scratch_shapes=[
-            pltpu.VMEM((2, rows, width), bf16), pltpu.VMEM(packed.shape, f32), pltpu.VMEM(tail.shape, f32),
-            dma((moves + 2,)), dma((moves + hidden // HS + 6,)),
+            pltpu.VMEM(packed.shape, f32), pltpu.VMEM(tail.shape, f32),
+            dma((2,)), dma((moves + hidden // HS + 6,)),
         ],
-        compiler_params=pltpu.CompilerParams(vmem_limit_bytes=62 * MIB),
+        compiler_params=pltpu.CompilerParams(vmem_limit_bytes=16 * MIB),
         name="finish",
-    )(gathered, gathered_grad, packed, tail)
+    )(
+        pltpu.with_memory_space_constraint(gathered, pltpu.VMEM),
+        pltpu.with_memory_space_constraint(gathered_grad, pltpu.VMEM),
+        pltpu.with_memory_space_constraint(packed, pltpu.HBM),
+        pltpu.with_memory_space_constraint(tail, pltpu.HBM),
+    )
 
 
 def local(
@@ -1047,7 +1088,7 @@
 ):
     norms = [vector.reshape(1, -1) for vector in (ln1_gain, ln1_bias, ln2_gain, ln2_bias)]
     w_qkv = jnp.transpose(qkv_master, (1, 0, 2))
-    gathered, gathered_grad, packed, tail, _ = whole(
+    _, _, packed, tail, gathered_grad, gathered = whole(
         lengths, tokens, cotangent, norms, w_qkv, qkv_bias, out_master, up_master,
         up_bias.reshape(1, -1), down_master, branch_bias.reshape(1, -1),
     )

time: 156 us -> 151 us (0.968)
  Pallas kernels: 155 us -> 149 us
    pallas_call x1, Pallas kernels: 8.29 us -> 4.63 us  [finish(): pl.pallas_call(finish_kernel, out_shape=(shape(gathered.shape, bf16), sha...]
    pallas_call x1, Pallas kernels: 146 us -> 145 us  [whole(): pl.pallas_call(whole_kernel, out_shape=outs, in_specs=[pl.BlockSpec(memor...]
where the time goes in v1:
time: 151 us; the launch traced here: 150 us
  Pallas kernels  149 us (99%)
    pallas_call x1, Pallas kernels, whole(): pl.pallas_call(whole_kernel, out_shape=outs, in_specs=[pl.BlockSpec(memor...  145 us
    pallas_call x1, Pallas kernels, finish(): pl.pallas_call(finish_kernel, out_shape=(shape(gathered.shape, bf16), sha...  4.63 us

profile of v1, /device:TPU:0, one launch (start us, length us, event | category | flops | bytes accessed | tf_op | source)
XLA Modules:
  0.0 150.2 jit_solution(8129408480821399225)
XLA Ops:
  0.7 144.8 %whole.1 = (bf16[1024,2048]{1,0:T(8,128)(2,1)}, bf16[1024,2048]{1,0:T(8,128)(2,1)}, f32[1536,256]{1,0:T(8,128)}, f32[8,1024]{1,0:T(8,128)}, bf16[1024,2048]{1,0:...) custom-call(s32[1,4]{1,0:T(1,128)} %lens.1, bf16[1024,2048]{1,0:T(8,128)(2,1)} %tok.1, bf16[1024,2048]{1,0:T(8,128)(2,1)} %cot.1, ...), custom_call_target="tpu_custom_call" | custom-call | tf_op jit(solution)/shard_map/whole/pallas_call | solution.py:988
  145.4 4.6 %finish.1 = (bf16[1024,2048]{1,0:T(8,128)(2,1)}, bf16[1024,2048]{1,0:T(8,128)(2,1)}, f32[128,1024]{1,0:T(8,128)}, f32[1024,128]{1,0:T(8,128)}, f32[3,128,256]{2,...) custom-call(bf16[1024,2048]{1,0:T(8,128)(2,1)S(1)} %get-tuple-elemen, ...), custom_call_target="tpu_custom_call" | custom-call | tf_op jit(solution)/shard_map/finish/pallas_call | solution.py:1061

commit v2 on v1

--- a/solution.py
+++ b/solution.py
@@ -326,11 +326,17 @@
     def pass_far(self):
         self.far.pass_on()
 
+    def arrive(self):
+        self.far.rest()
+        for link in self.across[1:4]:
+            link.got()
+
+    def arrive_opposite(self):
+        self.far.opposite()
+        for link in self.across[4:]:
+            link.got()
+
     def finish(self):
-        self.far.rest()
-        self.far.opposite()
-        for link in self.across[1:]:
-            link.got()
         for link in self.across:
             link.sent()
         self.near.finish()
@@ -839,12 +845,14 @@
     out_done = pltpu.make_async_copy(out, e_v, local_sems.at[5])
 
     def gt_copies(x_hi, first_sem):
-        parts = [aligned(y * BLK + x_hi * HALF, HALF) for y in range(4)]
+        parts = [aligned(here.y_at(off) * BLK + x_hi * HALF, HALF) for off in range(4)]
         return [pltpu.make_async_copy(gt.at[part], b_v.at[part], local_sems.at[first_sem + i]) for i, part in enumerate(parts)]
 
     gt_near, gt_far = gt_copies(here.x_hi, 6), gt_copies(1 - here.x_hi, 10)
 
     def finish_out():
+        gather_out.arrive()
+        gather_out.arrive_opposite()
         gather_out.finish()
         gather_out.keep.wait()
         out_done.start()
@@ -935,9 +943,12 @@
     one.finish()
     two.finish()
     small.finish()
+    gather_gt.arrive()
+    for off in (0, 1, 3):
+        gt_far[off].start()
+    gather_gt.arrive_opposite()
+    gt_far[2].start()
     gather_gt.finish()
-    for copy in gt_far:
-        copy.start()
     for copy in [tail_out, packed_out, out_done] + gt_near + gt_far:
         copy.wait()
 

time: 151 us -> 150 us (level)
  no operation moved by 1% of the time
where the time goes in v2:
time: 150 us
  Pallas kernels  149 us (99%)
    pallas_call x1, Pallas kernels, whole(): pl.pallas_call(whole_kernel, out_shape=outs, in_specs=[pl.BlockSpec(memor...  144 us
    pallas_call x1, Pallas kernels, finish(): pl.pallas_call(finish_kernel, out_shape=(shape(gathered.shape, bf16), sha...  4.63 us

profile of v2, /device:TPU:0, one launch (start us, length us, event | category | flops | bytes accessed | tf_op | source)
XLA Modules:
  0.0 149.7 jit_solution(18219490635015278197)
XLA Ops:
  0.7 144.2 %whole.1 = (bf16[1024,2048]{1,0:T(8,128)(2,1)}, bf16[1024,2048]{1,0:T(8,128)(2,1)}, f32[1536,256]{1,0:T(8,128)}, f32[8,1024]{1,0:T(8,128)}, bf16[1024,2048]{1,0:...) custom-call(s32[1,4]{1,0:T(1,128)} %lens.1, bf16[1024,2048]{1,0:T(8,128)(2,1)} %tok.1, bf16[1024,2048]{1,0:T(8,128)(2,1)} %cot.1, ...), custom_call_target="tpu_custom_call" | custom-call | tf_op jit(solution)/shard_map/whole/pallas_call | solution.py:999
  144.9 4.6 %finish.1 = (bf16[1024,2048]{1,0:T(8,128)(2,1)}, bf16[1024,2048]{1,0:T(8,128)(2,1)}, f32[128,1024]{1,0:T(8,128)}, f32[1024,128]{1,0:T(8,128)}, f32[3,128,256]{2,...) custom-call(bf16[1024,2048]{1,0:T(8,128)(2,1)S(1)} %get-tuple-elemen, ...), custom_call_target="tpu_custom_call" | custom-call | tf_op jit(solution)/shard_map/finish/pallas_call | solution.py:1072
